TPU v7x, 32 devices: a whole 2x2x4 slice. The times are simulated.
32 devices in a mesh: row: 8 (over z, x), col: 4 (over y, core).
Axes of the slice: x: 2, y: 2, z: 4, core: 2. Of those that a mesh axis runs over, the one named last changes fastest.
Arguments:
- front_tiles: bfloat16 [4, 2048, 2, 1024], P(None, 'row', None, 'col'), may hold values from -6 to 6
- fill_pattern: int32 [4, 8, 2, 4], P(None, 'row', None, 'col'), may hold values from 0 to 1
- w_inverse: bfloat16 [2, 256, 256], replicated, may hold values from -0.015625 to 0.015625
- samples: bfloat16 [4, 2048, 512], P(None, 'row'), may hold values from -6 to 6
Outputs:
- factor_slab: bfloat16 [4, 2048, 2, 1024], P(None, 'row', None, 'col')
- solved_rows: bfloat16 [4, 2048, 512], P(None, 'row')
All inputs are finite; a program needn't handle non-finite values.
Results may differ from a plain program's by a relative error of at most 0.0062.
Values may be sent and summed in bfloat16 or wider, within the bound.
A program may use at most 64 MiB of HBM per device.

v0:
```python
import jax
import jax.numpy as jnp
from jax import lax
from jax.sharding import PartitionSpec as P


def broadcast(block, axis, holder):
    block = jnp.where(lax.axis_index(axis) == holder, block, jnp.zeros_like(block))
    return lax.psum(block, axis)


def share_samples(tiles, root):
    return broadcast(tiles, "row", root)


def column_tiles(rows, cols_here):
    row_count = lax.axis_size("row")
    col_count = lax.axis_size("col")
    col_pos = lax.axis_index("col")
    pieces = []
    for place in range(cols_here):
        wanted = place * col_count + col_pos
        holder = wanted % row_count
        local_at = wanted // row_count
        held_tile = lax.dynamic_index_in_dim(rows, local_at, 0, keepdims=False)
        pieces.append(broadcast(held_tile, "row", holder))
    return jnp.stack(pieces)


def body(front_tiles, fill_pattern, w_inverse, samples):
    rows_here = front_tiles.shape[0]
    cols_here = front_tiles.shape[2]
    row_count = lax.axis_size("row")
    row_pos = lax.axis_index("row")
    col_pos = lax.axis_index("col")
    tile_row = jnp.arange(rows_here) * row_count + row_pos
    pattern = fill_pattern.astype(jnp.bfloat16)
    masked = front_tiles * pattern
    own_first = masked[:, :, 0, :]
    raw_zero = broadcast(own_first, "col", 0)
    raw_one = broadcast(own_first, "col", 1)
    first_panel = jnp.einsum(
        "akm,mn->akn", raw_zero, w_inverse[0], preferred_element_type=jnp.float32
    )
    first_panel = jnp.where(tile_row[:, None, None] >= 1, first_panel, 0.0).astype(jnp.bfloat16)
    lead_one = broadcast(first_panel[0], "row", 1)
    updated_second = raw_one.astype(jnp.float32) - jnp.einsum(
        "akm,nm->akn", first_panel, lead_one, preferred_element_type=jnp.float32
    )
    updated_second = updated_second.astype(jnp.bfloat16)
    second_panel = jnp.einsum(
        "akm,mn->akn", updated_second, w_inverse[1], preferred_element_type=jnp.float32
    )
    second_panel = jnp.where(tile_row[:, None, None] >= 2, second_panel, 0.0).astype(jnp.bfloat16)
    first_cols = column_tiles(first_panel, cols_here)
    second_cols = column_tiles(second_panel, cols_here)
    both_rows = jnp.concatenate([first_panel, second_panel], axis=2)
    both_cols = jnp.concatenate([first_cols, second_cols], axis=2)
    product = jnp.einsum("akm,bnm->akbn", both_rows, both_cols, preferred_element_type=jnp.float32)
    trailing = ((masked.astype(jnp.float32) - product) * pattern.astype(jnp.float32)).astype(
        jnp.bfloat16
    )
    first_lead = jnp.where(tile_row[:, None, None] >= 1, first_panel, own_first)
    second_lead = jnp.where(tile_row[:, None, None] >= 2, second_panel, updated_second)
    lead_tiles = jnp.where(
        col_pos == 0, first_lead, jnp.where(col_pos == 1, second_lead, trailing[:, :, 0, :])
    )
    factor_slab = trailing.at[:, :, 0, :].set(lead_tiles)
    first_local = jnp.einsum(
        "mn,ms->ns", w_inverse[0], samples[0], preferred_element_type=jnp.float32
    )
    first_solve = share_samples(first_local.astype(jnp.bfloat16), 0)
    reduced = (
        samples[0].astype(jnp.float32)
        - jnp.dot(first_panel[0], first_solve, preferred_element_type=jnp.float32)
    ).astype(jnp.bfloat16)
    second_local = jnp.einsum(
        "mn,ms->ns", w_inverse[1], reduced, preferred_element_type=jnp.float32
    )
    second_solve = share_samples(second_local.astype(jnp.bfloat16), 1)
    stacked = jnp.concatenate([first_solve, second_solve], axis=0)
    remaining = samples.astype(jnp.float32) - jnp.einsum(
        "akm,ms->aks", both_rows, stacked, preferred_element_type=jnp.float32
    )
    remaining = remaining.astype(jnp.bfloat16)
    top_rows = jnp.where(
        row_pos == 0, first_solve, jnp.where(row_pos == 1, second_solve, remaining[0])
    )
    solved_rows = remaining.at[0].set(top_rows)
    return (factor_slab, solved_rows)


def solution(mesh):
    in_specs = (P(None, "row", None, "col"), P(None, "row", None, "col"), P(), P(None, "row", None))
    out_specs = (P(None, "row", None, "col"), P(None, "row", None))
    return jax.shard_map(body, mesh=mesh, in_specs=in_specs, out_specs=out_specs, check_vma=False)
```

profile of v0, /device:TPU:7, one launch (start us, length us, event | category | flops | bytes accessed | tf_op | source)
XLA Modules:
  0.0 216.1 jit_solution(9891730402585357222)
XLA Ops:
  7.2 0.0 all-reduce.11.cloned.1.call-start
  7.2 0.7 convert_element_type.41
  7.9 1.4 copy_multiply_fusion
  9.3 0.0 copy-start.6
  9.3 1.0 broadcast_select_fusion
  10.4 0.0 all-reduce.11.cloned.1.call-update
  10.4 0.0 all-reduce.9.cloned.1.call-start
  10.4 0.0 copy-done.6
  10.5 1.9 fusion.4
  12.4 35.3 %all-reduce.11.cloned.1.call-done = (bf16[4,256,256]{2,1,0:T(8,128)(2,1)}, bf16[4,256,256]{2,1,0:T(8,128)(2,1)}) async-done(((bf16[4,256,256]{2,1,0:T(8,128)(2,1)}, bf16[4,256,256]{2,1,0:T(8,128)(2,1)}), (bf16[4,256,256]{2,1,0:T(8,128)(2,1)}, bf16[4,256,256]{2,1,0:T(8,128)(2,1)})) %all-reduce.11.cloned.1.call-update) | async-done | bytes 1048592 | tf_op jit(solution)/shard_map/psum | solution.py:9
  47.7 1.3 fusion.1
  49.0 0.7 broadcast_select_fusion.2
  49.7 0.0 all-reduce.9.cloned.1.call-update
  49.7 0.0 all-reduce.7.cloned.1.call-start
  49.8 0.7 dynamic-slice_select_fusion.3
  50.6 71.8 %all-reduce.9.cloned.1.call-done = (bf16[256,256]{1,0:T(8,128)(2,1)}, bf16[256,512]{1,0:T(8,128)(2,1)}) async-done(((bf16[256,256]{1,0:T(8,128)(2,1)}, bf16[256,512]{1,0:T(8,128)(2,1)}), (bf16[256,256]{1,0:T(8,128)(2,1)}, bf16[256,512]{1,0:T(8,128)(2,1)})) %all-reduce.9.cloned.1.call-update) | async-done | bytes 393232 | tf_op jit(solution)/shard_map/psum | solution.py:9
  122.4 2.2 %fusion.6 = bf16[256,512]{1,0:T(8,128)(2,1)} fusion(bf16[256,512]{1,0:T(8,128)(2,1)} %get-tuple-element.34, pred[]{:T(512)S(6)} %eq.32, bf16[4,256,512]{2,1,0:T(8,128)(2,1)} %param.11, bf16[4,256,256]{2,1,0:T(8,128)(2,1)S(1)} %fusion.1, bf16[2,256,256]{2,1,0:T(8,128)(2,1)S(1)} %copy-done.6), kind=kOutput, calls=%fused_computation.14 | convolution fusion | flops 134873088 | bytes 1048577 | tf_op jit(solution)/shard_map/mn,ms->ns/dot_general | solution.py:77
  124.6 0.3 fusion
  124.9 0.3 fusion.2
  125.2 0.7 dynamic-slice_select_fusion.1
  126.0 0.0 all-reduce.7.cloned.1.call-update
  126.0 77.4 %all-reduce.7.cloned.1.call-done = (bf16[1,256,256]{2,1,0:T(8,128)(2,1)}, bf16[1,256,256]{2,1,0:T(8,128)(2,1)}, bf16[1,256,256]{2,1,0:T(8,128)(2,1)}, bf16[1,256,256]{2,1,0:T(8,128)(2,1)}, bf16[256,512]{1,0:T(8,128)(2,1)}) async-done(((bf16[1,256,256]{2,1,0:T(8,128)(2,1)}, bf16[1,256,256]{2,1,0:T(8,128)(2,1)}, bf16[1,256,256]{2,1,0:T(8,128)(2,1)}, bf16[1,256,256]{2,1,0:T(8,128)(2,1)}, ...) | async-done | bytes 786448 | tf_op jit(solution)/shard_map/psum | solution.py:9
  203.4 1.8 multiply_convert_fusion
  205.2 0.0 copy-start.5
  205.2 0.6 fusion.11
  205.8 0.3 copy-done.1
  206.2 0.1 copy-done.2
  206.2 0.4 copy-done.5
  206.6 0.7 subtract_convert_fusion
  207.3 0.1 fusion.24
  207.5 0.0 copy-start.4
  207.5 2.0 copy.13
  (10 shorter events, 0.0 us)
Async XLA Ops:
  7.2 40.5 %all-reduce.11.cloned.1.call-start = ((), (), s32[]{:S(2)}) async-start(), calls=%async_computation.2 | async-start | bytes 2097152 | tf_op jit(solution)/shard_map/psum | solution.py:9
  9.3 1.2 copy-start.6
  10.4 112.0 %all-reduce.9.cloned.1.call-start = ((), (), s32[]{:S(2)}) async-start(), calls=%async_computation.1 | async-start | bytes 786432 | tf_op jit(solution)/shard_map/psum | solution.py:9
  49.7 74.9 %copy-start = (bf16[4,256,256]{2,1,0:T(8,128)(2,1)S(1)}, bf16[4,256,256]{2,1,0:T(8,128)(2,1)}, u32[]{:S(2)}) copy-start(bf16[4,256,256]{2,1,0:T(8,128)(2,1)} %get-tuple-element.36) | copy-start | bytes 1572868
  49.7 153.6 %all-reduce.7.cloned.1.call-start = ((), (), s32[]{:S(2)}) async-start(), calls=%async_computation | async-start | bytes 1572864 | tf_op jit(solution)/shard_map/psum | solution.py:9
  122.4 2.2 %copy-start.3 = (bf16[256,256]{1,0:T(8,128)(2,1)S(1)}, bf16[256,256]{1,0:T(8,128)(2,1)}, u32[]{:S(2)}) copy-start(bf16[256,256]{1,0:T(8,128)(2,1)} %get-tuple-element.33) | copy-start | bytes 393220
  205.2 1.0 copy-start.1
  205.2 1.0 copy-start.2
  205.2 1.4 copy-start.5
  207.5 2.1 copy-start.4
Sparse Core Ops, SparseCore 0:
  11.0 36.6 all-reduce.10
  52.0 70.3 all-reduce.8
  126.9 76.4 all-reduce.6
where the time goes:
time: 218 us; the launch traced here: 216 us
  waiting for transfers between devices  185 us (85%)
  between operations  13.9 us (6%)
  matrix products  8.62 us (4%)
  other arithmetic  6 us (3%)
  local copies, waits for them, and re-layouts  2.86 us (1%)
    psum x3, waiting for transfers between devices, broadcast(): return lax.psum(block, axis)  185 us
  transfers between devices with their start and end apart: 3, of which 3 were waited for; matrix products, arithmetic and copies ran while one was open for 1% of the time, Pallas kernels for 0%

commit v1 on v0

v1 whole, which is shorter than its diff:
```python
import functools

import jax
import jax.numpy as jnp
from jax import lax
from jax.experimental import pallas as pl
from jax.experimental.pallas import tpu as pltpu
from jax.sharding import PartitionSpec as P

MESH = pl.DeviceIdType.MESH
F32 = jnp.float32
BF16 = jnp.bfloat16


def dot_nn(a, b):
    return jnp.dot(a, b, preferred_element_type=F32)


def dot_nt(a, b):
    return lax.dot_general(a, b, (((1,), (1,)), ((), ())), preferred_element_type=F32)


def kernel(R, C, fm, w, smp, out, sol, rowf, colf, f10, sbuf, cols, rows, ys, l01,
           y_s, y_r, b_s, b_r, cu_s, cd_s, cx_s, c_r, fs_s, su_s, sx_s, sb_s, s_r, sb_r):
    A, TC, B, _ = fm.shape
    Q = R // 2
    Y = C // 2
    half = B // 2
    r, c = lax.axis_index("row"), lax.axis_index("col")
    q, x, yy, k = r // 2, r % 2, c // 2, c % 2
    sib = c + 1 - 2 * k
    mate = r + 1 - 2 * x
    pending = []

    def desc(src, dst, ss, rs, row, col):
        return pltpu.make_async_remote_copy(
            src_ref=src, dst_ref=dst, send_sem=ss, recv_sem=rs,
            device_id={"row": row, "col": col}, device_id_type=MESH)

    def send(cond, src, dst, ss, rs, row, col):
        copy = desc(src, dst, ss, rs, row, col)
        pending.append((cond, copy))

        @pl.when(cond)
        def _():
            copy.start()

    def arrive(cond, dst, rs):
        @pl.when(cond)
        def _():
            desc(dst, dst, fs_s.at[0], rs, r, sib).wait_recv()

    barrier = pltpu.get_barrier_semaphore()
    has_up, has_dn = q + 1 < Q, q > 0
    has_yu, has_yd = yy + 1 < Y, yy > 0
    true = r >= 0
    for cond, row, col in ((true, r, sib), (true, mate, c), (has_up, r + 2, c), (has_dn, r - 2, c),
                           (has_yu, r, c + 2), (has_yd, r, c - 2)):
        @pl.when(cond)
        def _():
            pl.semaphore_signal(barrier, inc=1, device_id={"row": row, "col": col}, device_id_type=MESH)
    ends = (q + 1 < Q).astype(jnp.int32) + (q > 0).astype(jnp.int32)
    ends = ends + (yy + 1 < Y).astype(jnp.int32) + (yy > 0).astype(jnp.int32)
    pl.semaphore_wait(barrier, 2 + ends)

    lead = yy == 0
    later = yy > 0

    for a in range(A):
        send(lead, fm.at[a, 0], rowf.at[k, a], b_s.at[a], b_r.at[a], r, sib)
        send(lead & has_yu, fm.at[a, 0], rowf.at[k, a], y_s.at[a], y_r.at[a], r, c + 2)

    mine = pl.ds(pl.multiple_of(k * half, half), half)
    other = pl.ds(pl.multiple_of((1 - k) * half, half), half)
    s_root = q == 0
    piece = smp.at[0, mine]
    send(s_root & has_up, piece, sbuf.at[x, mine], su_s.at[0], s_r.at[x], r + 2, c)
    send(s_root, piece, sbuf.at[x, mine], sx_s.at[0], s_r.at[x], mate, c)

    @pl.when(s_root)
    def _():
        sbuf[x] = smp[0]

    @pl.when(lead)
    def _():
        for a in range(A):
            rowf[k, a] = fm[a, 0]

    def row_tile(a):
        arrive(later, rowf.at[k, a], y_r.at[a])
        send(later, rowf.at[k, a], rowf.at[k, a], b_s.at[a], b_r.at[a], r, sib)
        send(later & has_yu, rowf.at[k, a], rowf.at[k, a], y_s.at[a], y_r.at[a], r, c + 2)

    def row_other(a):
        arrive(true, rowf.at[1 - k, a], b_r.at[a])

    line = x == k

    def root_of(b):
        return (b * C + c) % R

    def col_sends(cond, b, kk, qr):
        src = colf.at[b, kk]
        at = b * 2 + kk
        send(cond & line & has_up & (q >= qr), src, src, cu_s.at[at], c_r.at[at], r + 2, c)
        send(cond & line & has_dn & (q <= qr), src, src, cd_s.at[at], c_r.at[at], r - 2, c)
        send(cond & line, src, src, cx_s.at[at], c_r.at[at], mate, c)

    def col_item(b, kk):
        root = root_of(b)
        at = b * 2 + kk
        away = r != root
        arrive(away, colf.at[b, kk], c_r.at[at])
        col_sends(away, b, kk, root // 2)

    def col_roots(kk):
        for b in range(TC):
            root = root_of(b)

            @pl.when(r == root)
            def _():
                colf[b, kk] = rowf[kk, 0]
            col_sends(r == root, b, kk, root // 2)

    row_tile(0)
    col_roots(k)
    row_other(0)
    col_roots(1 - k)

    f_at = 2 * TC
    f_root = (r == 1) & (k == 1)
    f_line = (x == 1) & (k == 1)

    @pl.when(f_root)
    def _():
        f10[...] = rowf[0, 0]
    send(f_root & has_up, f10, f10, cu_s.at[f_at], c_r.at[f_at], r + 2, c)
    send(f_root, f10, f10, cx_s.at[f_at], c_r.at[f_at], mate, c)
    send(f_root, f10, f10, fs_s.at[0], c_r.at[f_at], r, sib)

    def sample_item(h, on_line):
        got = sbuf.at[h, mine]
        cond = (q > 0) if on_line else true
        arrive(cond, got, s_r.at[h])
        if on_line:
            send(cond & has_up, got, got, su_s.at[1], s_r.at[h], r + 2, c)
            send(cond, got, got, sx_s.at[1], s_r.at[h], mate, c)
        send(cond, got, got, sb_s.at[h], sb_r.at[h], r, sib)

    sample_item(x, True)

    if TC > 1:
        d0, d1 = jnp.abs(q - root_of(0) // 2), jnp.abs(q - root_of(1) // 2)
        first = jnp.where(d0 <= d1, 0, 1)
    else:
        first = 0
    col_item(first, k)
    col_item(first, 1 - k)
    if A > 1:
        row_tile(1)

    f_away = (k == 1) & (r != 1)
    arrive((k == 0) | f_away, f10, c_r.at[f_at])
    send(f_away & f_line & has_up, f10, f10, cu_s.at[f_at], c_r.at[f_at], r + 2, c)
    send(f_away & f_line, f10, f10, cx_s.at[f_at], c_r.at[f_at], mate, c)
    send(f_away, f10, f10, fs_s.at[0], c_r.at[f_at], r, sib)

    sample_item(1 - x, False)
    for t in range(1, TC):
        b = (first + t) % TC
        col_item(b, k)
        col_item(b, 1 - k)
    for a in range(2, A):
        row_tile(a)

    w0, w1 = w[0], w[1]
    l01[...] = dot_nn(f10[...], w0).astype(BF16)
    for b in range(TC):
        j = b * C + c
        f0 = (j >= 1).astype(F32)
        f1 = (j >= 2).astype(F32)
        c0 = (dot_nn(colf[b, 0], w0) * f0).astype(BF16)
        u = (colf[b, 1].astype(F32) - dot_nt(c0, l01[...])).astype(BF16)
        c1 = (dot_nn(u, w1) * f1).astype(BF16)
        cols[b, :, 0:B] = c0
        cols[b, :, B:2 * B] = c1

    arrive((q > 0) | (x != 0), sbuf.at[0, other], sb_r.at[0])
    arrive((q > 0) | (x != 1), sbuf.at[1, other], sb_r.at[1])
    w0t = w0.astype(F32).T.astype(BF16)
    w1t = w1.astype(F32).T.astype(BF16)
    y0 = dot_nn(w0t, sbuf[0]).astype(BF16)
    ys[0:B, :] = y0
    r1 = (sbuf[1].astype(F32) - dot_nn(l01[...], y0)).astype(BF16)
    ys[B:2 * B, :] = dot_nn(w1t, r1).astype(BF16)

    for a in range(1, A):
        row_other(a)

    def tile_row(a, carry):
        i = a * R + r
        f0 = (i >= 1).astype(F32)
        f1 = (i >= 2).astype(F32)
        p0 = (dot_nn(rowf[0, a], w[0]) * f0).astype(BF16)
        u = (rowf[1, a].astype(F32) - dot_nt(p0, l01[...])).astype(BF16)
        p1 = (dot_nn(u, w[1]) * f1).astype(BF16)
        rows[:, 0:B] = p0
        rows[:, B:2 * B] = p1
        for b in range(TC):
            out[a, b] = (fm[a, b].astype(F32) - dot_nt(rows[...], cols[b])).astype(BF16)
        sol[a] = (smp[a].astype(F32) - dot_nn(rows[...], ys[...])).astype(BF16)

        @pl.when((c == 0) & (i >= 1))
        def _():
            out[a, 0] = p0

        @pl.when((c == 0) & (i < 1))
        def _():
            out[a, 0] = rowf[0, a]

        @pl.when((c == 1) & (i >= 2))
        def _():
            out[a, 0] = p1

        @pl.when((c == 1) & (i < 2))
        def _():
            out[a, 0] = u

        @pl.when(i == 0)
        def _():
            sol[a] = ys[0:B, :]

        @pl.when(i == 1)
        def _():
            sol[a] = ys[B:2 * B, :]
        return carry

    lax.fori_loop(0, A, tile_row, 0)

    for cond, copy in pending:
        @pl.when(cond)
        def _():
            copy.wait_send()


def body(R, C, front_tiles, fill_pattern, w_inverse, samples):
    A, B, TC, _ = front_tiles.shape
    S = samples.shape[2]
    assert R % 2 == 0 and C % 2 == 0 and TC * C <= R and TC <= 2
    on = fill_pattern.reshape(A, 1, TC, 1) != 0
    zero = jnp.zeros((), BF16)
    fm = jnp.where(on, front_tiles, zero).transpose(0, 2, 1, 3)
    dma = pltpu.SemaphoreType.DMA
    vmem = pl.BlockSpec(memory_space=pltpu.VMEM)
    out, sol = pl.pallas_call(
        functools.partial(kernel, R, C),
        out_shape=(jax.ShapeDtypeStruct((A, TC, B, B), BF16), jax.ShapeDtypeStruct((A, B, S), BF16)),
        in_specs=[vmem] * 3,
        out_specs=(vmem, vmem),
        scratch_shapes=[
            pltpu.VMEM((2, A, B, B), BF16),
            pltpu.VMEM((TC, 2, B, B), BF16),
            pltpu.VMEM((B, B), BF16),
            pltpu.VMEM((2, B, S), BF16),
            pltpu.VMEM((TC, B, 2 * B), BF16),
            pltpu.VMEM((B, 2 * B), BF16),
            pltpu.VMEM((2 * B, S), BF16),
            pltpu.VMEM((B, B), BF16),
            dma((A,)), dma((A,)), dma((A,)), dma((A,)),
            dma((2 * TC + 1,)), dma((2 * TC + 1,)), dma((2 * TC + 1,)), dma((2 * TC + 1,)),
            dma((1,)), dma((2,)), dma((2,)), dma((2,)), dma((2,)), dma((2,)),
        ],
        compiler_params=pltpu.CompilerParams(
            collective_id=0, has_side_effects=True, vmem_limit_bytes=32 * 1024 * 1024),
        name="panels",
    )(fm, w_inverse, samples)
    factor = jnp.where(on, out.transpose(0, 2, 1, 3), zero)
    return factor, sol


def solution(mesh):
    R, C = mesh.shape["row"], mesh.shape["col"]
    in_specs = (P(None, "row", None, "col"), P(None, "row", None, "col"), P(), P(None, "row", None))
    out_specs = (P(None, "row", None, "col"), P(None, "row", None))
    return jax.shard_map(functools.partial(body, R, C), mesh=mesh, in_specs=in_specs,
                         out_specs=out_specs, check_vma=False)
```

time: 218 us -> 47 us (0.22)
  waiting for transfers between devices: 185 us -> 0 us
  Pallas kernels: 0 us -> 40.6 us
  between operations: 13.9 us -> 0.65 us
  matrix products: 8.62 us -> 0 us
  other arithmetic: 6 us -> 2.31 us
    psum x3 -> x0, waiting for transfers between devices: 185 us -> none  [broadcast(): return lax.psum(block, axis)]
    pallas_call x0 -> x1, Pallas kernels: none -> 40.6 us  [body(): pl.pallas_call(functools.partial(kernel, R, C), out_shape=(jax.ShapeDtype...]
    dot_general x7 -> x0, matrix products: 8.62 us -> none  [the longest x1 2.19 us: body(): jnp.einsum('mn,ms->ns', w_inverse[1], reduced, preferred_element_type=jnp...]
    select_n x4 -> x1, other arithmetic: 3.18 us -> 0.14 us  [body(): factor = jnp.where(on, out.transpose(0, 2, 1, 3), zero)]
  transfers between devices with their start and end apart: 3 -> 0, of which waited for: 3 -> 0; matrix products, arithmetic and copies ran while one was open for 1% -> 0% of each run, Pallas kernels for 0% -> 0%
where the time goes in v1:
time: 47 us; the launch traced here: 46.8 us
  Pallas kernels  40.6 us (86%)
  local copies, waits for them, and re-layouts  3.22 us (7%)
  other arithmetic  2.31 us (5%)
  between operations  0.65 us (1%)
    pallas_call x1, Pallas kernels, body(): pl.pallas_call(functools.partial(kernel, R, C), out_shape=(jax.ShapeDtype...  40.6 us
    unnamed x6, local copies, waits for them, and re-layouts  3.11 us
    transpose x1, other arithmetic, body(): fm = jnp.where(on, front_tiles, zero).transpose(0, 2, 1, 3)  1.49 us

profile of v1, /device:TPU:7, one launch (start us, length us, event | category | flops | bytes accessed | tf_op | source)
XLA Modules:
  0.0 46.8 jit_solution(16115282954612785531)
XLA Ops:
  0.6 0.7 %broadcast_compare_fusion = pred[4,1,2,1]{0,3,2,1:T(4,128)(4,1)S(1)} fusion(s32[4,1,2,1]{0,3,2,1:T(1,128)} %param.5), kind=kLoop, calls=%fused_computation.3 | loop fusion | flops 8 | bytes 40 | tf_op jit(solution)/shard_map/ne | solution.py:250
  1.3 0.1 copy.6
  1.4 0.0 copy-start
  1.4 0.0 copy-start.1
  1.4 1.5 %fusion.fm = bf16[4,2,256,256]{3,2,1,0:T(8,128)(2,1)S(1)} fusion(bf16[4,256,2,256]{3,2,1,0:T(2,128)(2,1)} %param.4, pred[4,2]{1,0:T(4,128)(4,1)S(1)} %bitcast.5), kind=kLoop, calls=%fused_computation.1 | loop fusion | flops 524288 | bytes 2097160 | tf_op jit(solution)/shard_map/transpose | solution.py:252
  2.9 0.0 copy-done
  3.0 0.0 copy-done.1
  3.0 40.6 %panels.1 = (bf16[4,2,256,256]{3,2,1,0:T(8,128)(2,1)S(1)}, bf16[4,256,512]{2,1,0:T(8,128)(2,1)S(1)}) custom-call(bf16[4,2,256,256]{3,2,1,0:T(8,128)(2,1)S(1)} %fusion.fm, bf16[2,256,256]{2,1,0:T(8,128)(2,1)S(1)} %copy-done.1, bf16[4,256,512]{2,1,0:T(8,128)(2,1)S(1)} %copy-done), custom_call_target="tpu_custom_call" | custom-call | tf_op jit(solution)/shard_map/panels/pallas_call | solution.py:255
  43.6 0.1 select_bitcast_fusion
  43.8 2.0 %copy.8 = bf16[4,256,2,256]{3,2,1,0:T(2,128)(2,1)} copy(bf16[4,256,2,256]{3,1,2,0:T(8,128)(2,1)S(1)} %select_bitcast_fusion) | data formatting | bytes 2097152
  45.8 1.0 %copy.13 = bf16[4,256,512]{2,1,0:T(8,128)(2,1)} copy(bf16[4,256,512]{2,1,0:T(8,128)(2,1)S(1)} %get-tuple-element.11) | data formatting | bytes 2097152
Async XLA Ops:
  1.4 1.5 %copy-start = (bf16[4,256,512]{2,1,0:T(8,128)(2,1)S(1)}, bf16[4,256,512]{2,1,0:T(8,128)(2,1)}, u32[]{:S(2)}) copy-start(bf16[4,256,512]{2,1,0:T(8,128)(2,1)} %smp.1) | copy-start | bytes 3145732
  1.4 1.6 %copy-start.1 = (bf16[2,256,256]{2,1,0:T(8,128)(2,1)S(1)}, bf16[2,256,256]{2,1,0:T(8,128)(2,1)}, u32[]{:S(2)}) copy-start(bf16[2,256,256]{2,1,0:T(8,128)(2,1)} %w.1) | copy-start | bytes 786436

commit v2 on v1

--- a/solution.py
+++ b/solution.py
@@ -21,7 +21,7 @@
 
 
 def kernel(R, C, fm, w, smp, out, sol, rowf, colf, f10, sbuf, cols, rows, ys, l01,
-           y_s, y_r, b_s, b_r, cu_s, cd_s, cx_s, c_r, fs_s, su_s, sx_s, sb_s, s_r, sb_r):
+           y_s, y_r, b_s, b_r, cz_s, cx_s, c_r, fz_s, fx_s, f_r, sz_s, s_s, s_r, sb_r):
     A, TC, B, _ = fm.shape
     Q = R // 2
     Y = C // 2
@@ -30,6 +30,7 @@
     q, x, yy, k = r // 2, r % 2, c // 2, c % 2
     sib = c + 1 - 2 * k
     mate = r + 1 - 2 * x
+    line_col = 2 * yy + x
     pending = []
 
     def desc(src, dst, ss, rs, row, col):
@@ -48,43 +49,45 @@
     def arrive(cond, dst, rs):
         @pl.when(cond)
         def _():
-            desc(dst, dst, fs_s.at[0], rs, r, sib).wait_recv()
+            desc(dst, dst, fx_s.at[0], rs, r, sib).wait_recv()
+
+    step = [jnp.where(2 * q < Q, Q - d, d) for d in range(1, Q)]
+    away_rows = [2 * lax.rem(q + d, Q) + x for d in step]
 
     barrier = pltpu.get_barrier_semaphore()
-    has_up, has_dn = q + 1 < Q, q > 0
     has_yu, has_yd = yy + 1 < Y, yy > 0
     true = r >= 0
-    for cond, row, col in ((true, r, sib), (true, mate, c), (has_up, r + 2, c), (has_dn, r - 2, c),
-                           (has_yu, r, c + 2), (has_yd, r, c - 2)):
+    peers = [(true, r, sib), (true, mate, c), (true, mate, sib), (has_yu, r, c + 2), (has_yd, r, c - 2)]
+    for row in away_rows:
+        peers += [(true, row, c), (true, row, sib)]
+    for cond, row, col in peers:
         @pl.when(cond)
         def _():
             pl.semaphore_signal(barrier, inc=1, device_id={"row": row, "col": col}, device_id_type=MESH)
-    ends = (q + 1 < Q).astype(jnp.int32) + (q > 0).astype(jnp.int32)
-    ends = ends + (yy + 1 < Y).astype(jnp.int32) + (yy > 0).astype(jnp.int32)
-    pl.semaphore_wait(barrier, 2 + ends)
+    ends = (yy + 1 < Y).astype(jnp.int32) + (yy > 0).astype(jnp.int32)
+    pl.semaphore_wait(barrier, 3 + 2 * (Q - 1) + ends)
 
     lead = yy == 0
     later = yy > 0
 
     for a in range(A):
-        send(lead, fm.at[a, 0], rowf.at[k, a], b_s.at[a], b_r.at[a], r, sib)
         send(lead & has_yu, fm.at[a, 0], rowf.at[k, a], y_s.at[a], y_r.at[a], r, c + 2)
 
-    mine = pl.ds(pl.multiple_of(k * half, half), half)
-    other = pl.ds(pl.multiple_of((1 - k) * half, half), half)
-    s_root = q == 0
-    piece = smp.at[0, mine]
-    send(s_root & has_up, piece, sbuf.at[x, mine], su_s.at[0], s_r.at[x], r + 2, c)
-    send(s_root, piece, sbuf.at[x, mine], sx_s.at[0], s_r.at[x], mate, c)
-
-    @pl.when(s_root)
-    def _():
-        sbuf[x] = smp[0]
-
     @pl.when(lead)
     def _():
-        for a in range(A):
-            rowf[k, a] = fm[a, 0]
+        rowf[k, 0] = fm[0, 0]
+
+    root_b = r // C
+    root = (r < TC * C) & ((r % C) // 2 == yy)
+    put_b = jnp.where(root, root_b, 0)
+    put = colf.at[put_b, k]
+    put_sem = c_r.at[put_b * 2 + k]
+    f_root = later & (r == 1) & (k == 0)
+
+    def root_sends(cond):
+        for n, row in enumerate(away_rows):
+            send(cond & root, rowf.at[k, 0], put, cz_s.at[n], put_sem, row, line_col)
+        send(cond & root, rowf.at[k, 0], put, cz_s.at[Q - 1], put_sem, mate, line_col)
 
     def row_tile(a):
         arrive(later, rowf.at[k, a], y_r.at[a])
@@ -94,84 +97,85 @@
     def row_other(a):
         arrive(true, rowf.at[1 - k, a], b_r.at[a])
 
-    line = x == k
-
-    def root_of(b):
-        return (b * C + c) % R
-
-    def col_sends(cond, b, kk, qr):
-        src = colf.at[b, kk]
-        at = b * 2 + kk
-        send(cond & line & has_up & (q >= qr), src, src, cu_s.at[at], c_r.at[at], r + 2, c)
-        send(cond & line & has_dn & (q <= qr), src, src, cd_s.at[at], c_r.at[at], r - 2, c)
-        send(cond & line, src, src, cx_s.at[at], c_r.at[at], mate, c)
-
-    def col_item(b, kk):
-        root = root_of(b)
-        at = b * 2 + kk
-        away = r != root
-        arrive(away, colf.at[b, kk], c_r.at[at])
-        col_sends(away, b, kk, root // 2)
-
-    def col_roots(kk):
-        for b in range(TC):
-            root = root_of(b)
-
-            @pl.when(r == root)
-            def _():
-                colf[b, kk] = rowf[kk, 0]
-            col_sends(r == root, b, kk, root // 2)
+    root_sends(lead)
+    for a in range(A):
+        send(lead, fm.at[a, 0], rowf.at[k, a], b_s.at[a], b_r.at[a], r, sib)
+
+    mine = pl.ds(pl.multiple_of(k * half, half), half)
+    other = pl.ds(pl.multiple_of((1 - k) * half, half), half)
+    top = yy == Y - 1
+    s_root = q == 0
+    piece = smp.at[0, mine]
+    for n, row in enumerate(away_rows):
+        send(s_root & top, piece, sbuf.at[x, mine], sz_s.at[n], s_r.at[x], row, c)
+    send(s_root, piece, sbuf.at[x, mine], s_s.at[0], s_r.at[x], mate, c)
+
+    @pl.when(s_root)
+    def _():
+        sbuf[x] = smp[0]
+
+    @pl.when(lead)
+    def _():
+        for a in range(1, A):
+            rowf[k, a] = fm[a, 0]
 
     row_tile(0)
-    col_roots(k)
+    root_sends(later)
+
+    for n, row in enumerate(away_rows):
+        send(f_root, rowf.at[0, 0], f10, fz_s.at[n], f_r.at[0], row, c)
+    send(f_root, rowf.at[0, 0], f10, fx_s.at[0], f_r.at[0], mate, c)
+    send(f_root, rowf.at[0, 0], f10, fx_s.at[1], f_r.at[0], r, sib)
+
+    @pl.when(f_root)
+    def _():
+        f10[...] = rowf[0, 0]
+
+    def sample_own(cond):
+        got = sbuf.at[x, mine]
+        cond = cond & (q > 0)
+        arrive(cond, got, s_r.at[x])
+        send(cond, got, got, s_s.at[1], s_r.at[x], mate, c)
+        send(cond & has_yd, got, got, s_s.at[2], s_r.at[x], r, c - 2)
+        send(cond, got, got, s_s.at[3], sb_r.at[x], r, sib)
+
+    for a in range(1, min(A, 2)):
+        row_tile(a)
+    sample_own(later)
+    for a in range(2, min(A, 3)):
+        row_tile(a)
+
+    f_got = later & (k == 0) & (r != 1)
+    arrive(f_got, f10, f_r.at[0])
+    send(f_got & (x == 1), f10, f10, fx_s.at[2], f_r.at[0], mate, c)
+    send(f_got, f10, f10, fx_s.at[3], f_r.at[0], r, sib)
+    arrive(later & (k == 1), f10, f_r.at[0])
+    for a in range(3, A):
+        row_tile(a)
+
     row_other(0)
-    col_roots(1 - k)
-
-    f_at = 2 * TC
-    f_root = (r == 1) & (k == 1)
-    f_line = (x == 1) & (k == 1)
-
-    @pl.when(f_root)
-    def _():
-        f10[...] = rowf[0, 0]
-    send(f_root & has_up, f10, f10, cu_s.at[f_at], c_r.at[f_at], r + 2, c)
-    send(f_root, f10, f10, cx_s.at[f_at], c_r.at[f_at], mate, c)
-    send(f_root, f10, f10, fs_s.at[0], c_r.at[f_at], r, sib)
-
-    def sample_item(h, on_line):
-        got = sbuf.at[h, mine]
-        cond = (q > 0) if on_line else true
-        arrive(cond, got, s_r.at[h])
-        if on_line:
-            send(cond & has_up, got, got, su_s.at[1], s_r.at[h], r + 2, c)
-            send(cond, got, got, sx_s.at[1], s_r.at[h], mate, c)
-        send(cond, got, got, sb_s.at[h], sb_r.at[h], r, sib)
-
-    sample_item(x, True)
-
-    if TC > 1:
-        d0, d1 = jnp.abs(q - root_of(0) // 2), jnp.abs(q - root_of(1) // 2)
-        first = jnp.where(d0 <= d1, 0, 1)
-    else:
-        first = 0
-    col_item(first, k)
-    col_item(first, 1 - k)
-    if A > 1:
-        row_tile(1)
-
-    f_away = (k == 1) & (r != 1)
-    arrive((k == 0) | f_away, f10, c_r.at[f_at])
-    send(f_away & f_line & has_up, f10, f10, cu_s.at[f_at], c_r.at[f_at], r + 2, c)
-    send(f_away & f_line, f10, f10, cx_s.at[f_at], c_r.at[f_at], mate, c)
-    send(f_away, f10, f10, fs_s.at[0], c_r.at[f_at], r, sib)
-
-    sample_item(1 - x, False)
-    for t in range(1, TC):
-        b = (first + t) % TC
-        col_item(b, k)
-        col_item(b, 1 - k)
-    for a in range(2, A):
-        row_tile(a)
+    for b in range(TC):
+        row_b = (b * C + c) % R
+
+        @pl.when(r == row_b)
+        def _():
+            colf[b] = rowf[:, 0]
+        for kk in range(2):
+            at = b * 2 + kk
+            ref = colf.at[b, kk]
+            arrive(r != row_b, ref, c_r.at[at])
+            send((r != row_b) & (x == k), ref, ref, cx_s.at[at], c_r.at[at], mate, c)
+
+    @pl.when(lead & (k == 1))
+    def _():
+        f10[...] = colf[0, 0]
+    send(lead & (k == 1), colf.at[0, 0], f10, fx_s.at[4], f_r.at[0], r, sib)
+    arrive(lead & (k == 0), f10, f_r.at[0])
+
+    sample_own(lead)
+    got = sbuf.at[1 - x, mine]
+    arrive(true, got, s_r.at[1 - x])
+    send(true, got, got, s_s.at[4], sb_r.at[1 - x], r, sib)
 
     w0, w1 = w[0], w[1]
     l01[...] = dot_nn(f10[...], w0).astype(BF16)
@@ -185,8 +189,8 @@
         cols[b, :, 0:B] = c0
         cols[b, :, B:2 * B] = c1
 
-    arrive((q > 0) | (x != 0), sbuf.at[0, other], sb_r.at[0])
-    arrive((q > 0) | (x != 1), sbuf.at[1, other], sb_r.at[1])
+    arrive(q > 0, sbuf.at[x, other], sb_r.at[x])
+    arrive(true, sbuf.at[1 - x, other], sb_r.at[1 - x])
     w0t = w0.astype(F32).T.astype(BF16)
     w1t = w1.astype(F32).T.astype(BF16)
     y0 = dot_nn(w0t, sbuf[0]).astype(BF16)
@@ -267,8 +271,9 @@
             pltpu.VMEM((2 * B, S), BF16),
             pltpu.VMEM((B, B), BF16),
             dma((A,)), dma((A,)), dma((A,)), dma((A,)),
-            dma((2 * TC + 1,)), dma((2 * TC + 1,)), dma((2 * TC + 1,)), dma((2 * TC + 1,)),
-            dma((1,)), dma((2,)), dma((2,)), dma((2,)), dma((2,)), dma((2,)),
+            dma((R // 2,)), dma((2 * TC,)), dma((2 * TC,)),
+            dma((R // 2,)), dma((5,)), dma((1,)),
+            dma((R // 2,)), dma((5,)), dma((2,)), dma((2,)),
         ],
         compiler_params=pltpu.CompilerParams(
             collective_id=0, has_side_effects=True, vmem_limit_bytes=32 * 1024 * 1024),

time: 47 us -> 40.6 us (0.86)
  the two profiles are of different devices: /device:TPU:7 before, /device:TPU:23 now
where the time goes in v2:
time: 40.6 us; the launch traced here: 40.4 us
  Pallas kernels  34.2 us (84%)
  local copies, waits for them, and re-layouts  3.22 us (8%)
  other arithmetic  2.31 us (6%)
  between operations  0.65 us (2%)
    pallas_call x1, Pallas kernels, body(): pl.pallas_call(functools.partial(kernel, R, C), out_shape=(jax.ShapeDtype...  34.2 us
    unnamed x6, local copies, waits for them, and re-layouts  3.11 us
    transpose x1, other arithmetic, body(): fm = jnp.where(on, front_tiles, zero).transpose(0, 2, 1, 3)  1.49 us

profile of v2, /device:TPU:23, one launch (start us, length us, event | category | flops | bytes accessed | tf_op | source)
XLA Modules:
  0.0 40.4 jit_solution(1696855697565004057)
XLA Ops:
  0.6 0.7 %broadcast_compare_fusion = pred[4,1,2,1]{0,3,2,1:T(4,128)(4,1)S(1)} fusion(s32[4,1,2,1]{0,3,2,1:T(1,128)} %param.5), kind=kLoop, calls=%fused_computation.3 | loop fusion | flops 8 | bytes 40 | tf_op jit(solution)/shard_map/ne | solution.py:254
  1.3 0.1 copy.6
  1.4 0.0 copy-start
  1.4 0.0 copy-start.1
  1.4 1.5 %fusion.fm = bf16[4,2,256,256]{3,2,1,0:T(8,128)(2,1)S(1)} fusion(bf16[4,256,2,256]{3,2,1,0:T(2,128)(2,1)} %param.4, pred[4,2]{1,0:T(4,128)(4,1)S(1)} %bitcast.5), kind=kLoop, calls=%fused_computation.1 | loop fusion | flops 524288 | bytes 2097160 | tf_op jit(solution)/shard_map/transpose | solution.py:256
  2.9 0.0 copy-done
  3.0 0.0 copy-done.1
  3.0 34.2 %panels.1 = (bf16[4,2,256,256]{3,2,1,0:T(8,128)(2,1)S(1)}, bf16[4,256,512]{2,1,0:T(8,128)(2,1)S(1)}) custom-call(bf16[4,2,256,256]{3,2,1,0:T(8,128)(2,1)S(1)} %fusion.fm, bf16[2,256,256]{2,1,0:T(8,128)(2,1)S(1)} %copy-done.1, bf16[4,256,512]{2,1,0:T(8,128)(2,1)S(1)} %copy-done), custom_call_target="tpu_custom_call" | custom-call | tf_op jit(solution)/shard_map/panels/pallas_call | solution.py:259
  37.3 0.1 select_bitcast_fusion
  37.4 2.0 %copy.8 = bf16[4,256,2,256]{3,2,1,0:T(2,128)(2,1)} copy(bf16[4,256,2,256]{3,1,2,0:T(8,128)(2,1)S(1)} %select_bitcast_fusion) | data formatting | bytes 2097152
  39.5 1.0 %copy.13 = bf16[4,256,512]{2,1,0:T(8,128)(2,1)} copy(bf16[4,256,512]{2,1,0:T(8,128)(2,1)S(1)} %get-tuple-element.11) | data formatting | bytes 2097152
Async XLA Ops:
  1.4 1.5 %copy-start = (bf16[4,256,512]{2,1,0:T(8,128)(2,1)S(1)}, bf16[4,256,512]{2,1,0:T(8,128)(2,1)}, u32[]{:S(2)}) copy-start(bf16[4,256,512]{2,1,0:T(8,128)(2,1)} %smp.1) | copy-start | bytes 3145732
  1.4 1.6 %copy-start.1 = (bf16[2,256,256]{2,1,0:T(8,128)(2,1)S(1)}, bf16[2,256,256]{2,1,0:T(8,128)(2,1)}, u32[]{:S(2)}) copy-start(bf16[2,256,256]{2,1,0:T(8,128)(2,1)} %w.1) | copy-start | bytes 786436
